TPU v7x, 32 devices: a whole 2x2x4 slice. The times are simulated.
32 devices in a mesh: context: 16 (over z, y, x), fsdp: 2 (over core).
Axes of the slice: x: 2, y: 2, z: 4, core: 2. Of those that a mesh axis runs over, the one named last changes fastest.
Arguments:
- queries: bfloat16 [2, 2048, 2048], P('fsdp', 'context'), may hold values from -200 to 200, as said below
- keys: bfloat16 [2, 2048, 1024], P('fsdp', 'context'), may hold values from -20 to 20, as said below
- values: bfloat16 [2, 2048, 1024], P('fsdp', 'context'), may hold values from -6 to 6
- output_gradient: bfloat16 [2, 2048, 2048], P('fsdp', 'context'), may hold values from -48 to 48
- adapter_hidden: bfloat16 [2, 2048, 16], P('fsdp', 'context'), may hold values from -0.09375 to 0.09375
- counts: int32 [2, 16], P('fsdp', 'context'), may hold values from 112 to 128, as said below
- offsets: int32 [2, 16], P('fsdp', 'context'), may hold values from 0 to 1776, as said below
Outputs:
- grad_queries: bfloat16 [2, 2048, 2048], P('fsdp', 'context')
- grad_keys: bfloat16 [2, 2048, 1024], P('fsdp', 'context')
- value_gradient: bfloat16 [2, 2048, 1024], P('fsdp', 'context')
- adapter_grad: float32 [16, 1024], P(None, 'fsdp')
Inputs may be any that keep to these rules, and one draw needn't show every extreme that they name: `counts`: A shard's valid tokens fill its first slots. In every row some shard is full, and 9 consecutive shards, not starting at the first shard, hold 112 valid tokens each. offsets[row, s] is the sum of counts[row, r] over r < s. `queries`: finite values. `keys`: finite values.
All inputs are finite; a program needn't handle non-finite values.
Results may differ from a plain program's by a relative error of at most 0.01.
Values may be sent and summed in bfloat16 or wider, within the bound.
A program may use at most 64 MiB of HBM per device.

v0:
```python
import jax
import jax.numpy as jnp
from jax import lax
from jax.sharding import PartitionSpec as P

HQ = 16
KEY_VALUE_HEADS = 8
HEAD_SIZE = 128
WINDOW = 1024
REACH = 10


SCORE_SCALE = 168.0 ** (-0.5)
ADAPTER_SCALE = 2.0


def shifted(value, axis, steps):
    count = lax.axis_size(axis)
    initial, last = (max(0, -steps), min(count, count - steps))
    return lax.ppermute(value, axis, [(source, source + steps) for source in range(initial, last)])


def local(queries, keys, values, output_gradient, adapter_hidden, counts, offsets):
    present_rows = queries.shape[1]
    feature_columns = keys.shape[2]
    slot_ids = jnp.arange(present_rows, dtype=jnp.int32)
    own_offset = offsets[0, 0]
    own_count = counts[0, 0]
    valid_rows = slot_ids < own_count
    masked_scores = jnp.where(
        valid_rows[:, None], output_gradient[0], jnp.zeros_like(output_gradient[0])
    )
    query_quad_rows = queries[0].reshape(present_rows, KEY_VALUE_HEADS, 2, HEAD_SIZE)
    masked_quad_scores = masked_scores.reshape(present_rows, KEY_VALUE_HEADS, 2, HEAD_SIZE)
    own_items = (keys[0], values[0], offsets[0], counts[0])
    arrived = []
    current = own_items
    for hop_index in range(REACH):
        current = shifted((current[0], current[1], current[2], current[3]), "context", 1)
        arrived.append(current)
    window_items = arrived[::-1] + [own_items]
    key_complete = jnp.concatenate([shard_data[0] for shard_data in window_items], axis=0)
    value_complete = jnp.concatenate([shard_data[1] for shard_data in window_items], axis=0)
    key_pos = jnp.concatenate([shard_data[2][0] + slot_ids for shard_data in window_items], axis=0)
    key_ok = jnp.concatenate([slot_ids < shard_data[3][0] for shard_data in window_items], axis=0)
    total_keys = key_complete.shape[0]
    key_idx = jnp.arange(total_keys, dtype=jnp.int32)
    query_idx = REACH * present_rows + slot_ids
    query_pos = own_offset + slot_ids
    block_cap = 512
    block_list = []
    block_begin = 0
    while block_begin < total_keys:
        block_extent = min(block_cap, total_keys - block_begin)
        block_list.append((block_begin, block_extent))
        block_begin = block_begin + block_extent

    def block_scores(block_opening, block_extent):
        key_piece = key_complete[block_opening : block_opening + block_extent].reshape(
            block_extent, KEY_VALUE_HEADS, HEAD_SIZE
        )
        value_piece = value_complete[block_opening : block_opening + block_extent].reshape(
            block_extent, KEY_VALUE_HEADS, HEAD_SIZE
        )
        scores = (
            jnp.einsum(
                "tgjd,kgd->gjtk", query_quad_rows, key_piece, preferred_element_type=jnp.float32
            )
            * SCORE_SCALE
        )
        dprobs = jnp.einsum(
            "tgjd,kgd->gjtk", masked_quad_scores, value_piece, preferred_element_type=jnp.float32
        )
        return (scores, dprobs)

    statistic_shape = (KEY_VALUE_HEADS, 2, present_rows)
    stats = (
        jnp.full(statistic_shape, -1e30, jnp.float32),
        jnp.zeros(statistic_shape, jnp.float32),
        jnp.zeros(statistic_shape, jnp.float32),
    )
    allowed_list = []
    for block_opening, block_extent in block_list:
        tile_pos = key_pos[block_opening : block_opening + block_extent]
        tile_ok = key_ok[block_opening : block_opening + block_extent]
        tile_idx = key_idx[block_opening : block_opening + block_extent]
        allowed = (
            tile_ok[None, :]
            & (tile_idx[None, :] <= query_idx[:, None])
            & (query_pos[:, None] - tile_pos[None, :] < WINDOW)
        )
        allowed_list.append(allowed)
        first_running_max, first_running_sum, first_running_dot = stats
        first_scores, first_dprobs = block_scores(block_opening, block_extent)
        live_scores = jnp.where(allowed, first_scores, -jnp.inf)
        new_max = jnp.maximum(first_running_max, jnp.max(live_scores, axis=-1))
        rescale = jnp.exp(first_running_max - new_max)
        weights = jnp.exp(live_scores - new_max[..., None])
        stats = (
            new_max,
            first_running_sum * rescale + jnp.sum(weights, axis=-1),
            first_running_dot * rescale + jnp.sum(weights * first_dprobs, axis=-1),
        )
    running_max, running_sum, running_dot = stats
    log_total = running_max + jnp.log(running_sum)
    row_delta = running_dot / running_sum
    query_accumulator = jnp.zeros((present_rows, KEY_VALUE_HEADS, 2, HEAD_SIZE), jnp.float32)
    key_blocks = []
    value_blocks = []
    for block_number in range(len(block_list)):
        block_opening, block_extent = block_list[block_number]
        allowed = allowed_list[block_number]
        second_key_piece = key_complete[block_opening : block_opening + block_extent].reshape(
            block_extent, KEY_VALUE_HEADS, HEAD_SIZE
        )
        second_scores, second_dprobs = block_scores(block_opening, block_extent)
        second_weights = jnp.where(allowed, jnp.exp(second_scores - log_total[..., None]), 0.0)
        half_weights = second_weights.astype(jnp.bfloat16)
        dscores = (second_weights * (second_dprobs - row_delta[..., None])).astype(jnp.bfloat16)
        query_part = jnp.einsum(
            "gjtk,kgd->tgjd", dscores, second_key_piece, preferred_element_type=jnp.float32
        )
        key_part = (
            jnp.einsum(
                "gjtk,tgjd->kgd", dscores, query_quad_rows, preferred_element_type=jnp.float32
            )
            * SCORE_SCALE
        ).astype(jnp.bfloat16)
        value_part = jnp.einsum(
            "gjtk,tgjd->kgd", half_weights, masked_quad_scores, preferred_element_type=jnp.float32
        ).astype(jnp.bfloat16)
        query_part, key_part, value_part = (
            query_part,
            key_part.reshape(block_extent, feature_columns),
            value_part.reshape(block_extent, feature_columns),
        )
        query_accumulator = query_accumulator + query_part
        key_blocks.append(key_part)
        value_blocks.append(value_part)
    key_terms = jnp.concatenate(key_blocks, axis=0).reshape(
        REACH + 1, present_rows, feature_columns
    )
    value_terms = jnp.concatenate(value_blocks, axis=0).reshape(
        REACH + 1, present_rows, feature_columns
    )
    key_sum = key_terms[REACH].astype(jnp.float32)
    value_sum = value_terms[REACH].astype(jnp.float32)
    for distance in range(1, REACH + 1):
        back_keys, back_values = shifted(
            (key_terms[REACH - distance], value_terms[REACH - distance]), "context", -distance
        )
        key_sum = key_sum + back_keys.astype(jnp.float32)
        value_sum = value_sum + back_values.astype(jnp.float32)
    grad_keys = key_sum.astype(jnp.bfloat16)
    value_gradient = value_sum.astype(jnp.bfloat16)
    grad_queries = (
        (query_accumulator * SCORE_SCALE)
        .astype(jnp.bfloat16)
        .reshape(1, present_rows, HQ * HEAD_SIZE)
    )
    adapter_term = ADAPTER_SCALE * jnp.einsum(
        "ud,ug->dg", adapter_hidden[0], value_gradient, preferred_element_type=jnp.float32
    )
    adapter_whole = lax.psum(adapter_term, "context")
    adapter_grad = lax.psum_scatter(adapter_whole, "fsdp", scatter_dimension=1, tiled=True)
    return (grad_queries, grad_keys[None], value_gradient[None], adapter_grad)


def solution(mesh):
    in_specs = (
        P("fsdp", "context", None),
        P("fsdp", "context", None),
        P("fsdp", "context", None),
        P("fsdp", "context", None),
        P("fsdp", "context", None),
        P("fsdp", "context"),
        P("fsdp", "context"),
    )
    out_specs = (
        P("fsdp", "context", None),
        P("fsdp", "context", None),
        P("fsdp", "context", None),
        P(None, "fsdp"),
    )
    return jax.shard_map(local, mesh=mesh, in_specs=in_specs, out_specs=out_specs, check_vma=False)
```

profile of v0, /device:TPU:0, one launch (start us, length us, event | category | flops | bytes accessed | tf_op | source)
XLA Modules:
  0.0 434.1 jit_solution(1895409355445478376)
XLA Ops:
  7.2 5.3 %collective-permute-start.20 = (s32[1]{0:T(128)}, s32[1]{0:T(128)}, u32[]{:S(2)}, u32[]{:S(2)}) collective-permute-start(s32[1]{0:T(128)} %bitcast.10), channel_id=1, source_target_pairs={{0,2},{2,4},{4,6},{6,8},{8,10},{10,12},{12,14},{14,16},{16,18},{18... | collective-permute-start | bytes 20 | tf_op jit(solution)/shard_map/ppermute | solution.py:20
  30.2 4.0 collective-permute-start.21
  39.3 4.8 %collective-permute-start.22 = (s32[1]{0:T(128)}, s32[1]{0:T(128)}, u32[]{:S(2)}, u32[]{:S(2)}) collective-permute-start(s32[1]{0:T(128)} %collective-permute-done.21), channel_id=1, source_target_pairs={{0,2},{2,4},{4,6},{6,8},{8,10},{10,12},{12,14},{14,16},{16,18},{18... | collective-permute-start | bytes 20 | tf_op jit(solution)/shard_map/ppermute | solution.py:20
  44.1 4.3 collective-permute-start.12
  50.9 5.2 %collective-permute-start.13 = (s32[1]{0:T(128)}, s32[1]{0:T(128)}, u32[]{:S(2)}, u32[]{:S(2)}) collective-permute-start(s32[1]{0:T(128)} %collective-permute-done.12), channel_id=1, source_target_pairs={{0,2},{2,4},{4,6},{6,8},{8,10},{10,12},{12,14},{14,16},{16,18},{18... | collective-permute-start | bytes 20 | tf_op jit(solution)/shard_map/ppermute | solution.py:20
  59.5 5.9 %collective-permute-start.24 = (s32[1]{0:T(128)}, s32[1]{0:T(128)}, u32[]{:S(2)}, u32[]{:S(2)}) collective-permute-start(s32[1]{0:T(128)} %collective-permute-done.23), channel_id=1, source_target_pairs={{0,2},{2,4},{4,6},{6,8},{8,10},{10,12},{12,14},{14,16},{16,18},{18... | collective-permute-start | bytes 20 | tf_op jit(solution)/shard_map/ppermute | solution.py:20
  75.0 6.0 %collective-permute-start.25 = (s32[1]{0:T(128)}, s32[1]{0:T(128)}, u32[]{:S(2)}, u32[]{:S(2)}) collective-permute-start(s32[1]{0:T(128)} %collective-permute-done.24), channel_id=1, source_target_pairs={{0,2},{2,4},{4,6},{6,8},{8,10},{10,12},{12,14},{14,16},{16,18},{18... | collective-permute-start | bytes 20 | tf_op jit(solution)/shard_map/ppermute | solution.py:20
  104.7 4.1 collective-permute-start.33
  128.0 5.0 %collective-permute-start.5 = (bf16[128,1024]{0,1:T(8,128)(2,1)S(1)}, bf16[128,1024]{0,1:T(8,128)(2,1)}, u32[]{:S(2)}, u32[]{:S(2)}) collective-permute-start(bf16[128,1024]{0,1:T(8,128)(2,1)S(1)} %collective-permute-done.4), channel_id=1, source_target_pairs={{0,2},{2,4},{4,6},{6,8},{8,10},{10,12},{12,14},{14,16},{16,18},{18... | collective-permute-start | bytes 786440 | tf_op jit(solution)/shard_map/ppermute | solution.py:20
  134.3 4.6 %collective-permute-start.35 = (bf16[128,1024]{0,1:T(8,128)(2,1)}, bf16[128,1024]{0,1:T(8,128)(2,1)}, u32[]{:S(2)}, u32[]{:S(2)}) collective-permute-start(bf16[128,1024]{0,1:T(8,128)(2,1)} %collective-permute-done.34), channel_id=1, source_target_pairs={{0,2},{2,4},{4,6},{6,8},{8,10},{10,12},{12,14},{14,16},{16,18},{18... | collective-permute-start | bytes 786440 | tf_op jit(solution)/shard_map/ppermute | solution.py:20
  139.1 5.5 %collective-permute-start.6 = (bf16[128,1024]{0,1:T(8,128)(2,1)}, bf16[128,1024]{0,1:T(8,128)(2,1)}, u32[]{:S(2)}, u32[]{:S(2)}) collective-permute-start(bf16[128,1024]{0,1:T(8,128)(2,1)} %collective-permute-done.5), channel_id=1, source_target_pairs={{0,2},{2,4},{4,6},{6,8},{8,10},{10,12},{12,14},{14,16},{16,18},{18... | collective-permute-start | bytes 786440 | tf_op jit(solution)/shard_map/ppermute | solution.py:20
  146.1 4.7 %collective-permute-start.36 = (bf16[128,1024]{0,1:T(8,128)(2,1)}, bf16[128,1024]{0,1:T(8,128)(2,1)S(1)}, u32[]{:S(2)}, u32[]{:S(2)}) collective-permute-start(bf16[128,1024]{0,1:T(8,128)(2,1)} %collective-permute-done.35), channel_id=1, source_target_pairs={{0,2},{2,4},{4,6},{6,8},{8,10},{10,12},{12,14},{14,16},{16,18},{18... | collective-permute-start | bytes 786440 | tf_op jit(solution)/shard_map/ppermute | solution.py:20
  150.9 5.4 %collective-permute-start.7 = (bf16[128,1024]{0,1:T(8,128)(2,1)}, bf16[128,1024]{0,1:T(8,128)(2,1)S(1)}, u32[]{:S(2)}, u32[]{:S(2)}) collective-permute-start(bf16[128,1024]{0,1:T(8,128)(2,1)} %collective-permute-done.6), channel_id=1, source_target_pairs={{0,2},{2,4},{4,6},{6,8},{8,10},{10,12},{12,14},{14,16},{16,18},{18... | collective-permute-start | bytes 786440 | tf_op jit(solution)/shard_map/ppermute | solution.py:20
  156.9 5.3 %collective-permute-start.37 = (bf16[128,1024]{0,1:T(8,128)(2,1)S(1)}, bf16[128,1024]{0,1:T(8,128)(2,1)S(1)}, u32[]{:S(2)}, u32[]{:S(2)}) collective-permute-start(bf16[128,1024]{0,1:T(8,128)(2,1)S(1)} %collective-permute-done.36), channel_id=1, source_target_pairs={{0,2},{2,4},{4,6},{6,8},{8,10},{10,12},{12,14},{14,16},{16,18},{18... | collective-permute-start | bytes 786440 | tf_op jit(solution)/shard_map/ppermute | solution.py:20
  163.3 4.3 collective-permute-start.8
  170.1 4.8 %collective-permute-start.38 = (bf16[128,1024]{0,1:T(8,128)(2,1)S(1)}, bf16[128,1024]{0,1:T(8,128)(2,1)S(1)}, u32[]{:S(2)}, u32[]{:S(2)}) collective-permute-start(bf16[128,1024]{0,1:T(8,128)(2,1)S(1)} %collective-permute-done.37), channel_id=1, source_target_pairs={{0,2},{2,4},{4,6},{6,8},{8,10},{10,12},{12,14},{14,16},{16,18},{18... | collective-permute-start | bytes 786440 | tf_op jit(solution)/shard_map/ppermute | solution.py:20
  179.4 5.0 %collective-permute-start.39 = (bf16[128,1024]{0,1:T(8,128)(2,1)S(1)}, bf16[128,1024]{0,1:T(8,128)(2,1)S(1)}, u32[]{:S(2)}, u32[]{:S(2)}) collective-permute-start(bf16[128,1024]{0,1:T(8,128)(2,1)S(1)} %collective-permute-done.38), channel_id=1, source_target_pairs={{0,2},{2,4},{4,6},{6,8},{8,10},{10,12},{12,14},{14,16},{16,18},{18... | collective-permute-start | bytes 786440 | tf_op jit(solution)/shard_map/ppermute | solution.py:20
  236.7 29.5 %collective-permute-done.48 = bf16[128,1024]{1,0:T(8,128)(2,1)} collective-permute-done((bf16[128,1024]{1,0:T(8,128)(2,1)}, bf16[128,1024]{1,0:T(8,128)(2,1)}, u32[]{:S(2)}, u32[]{:S(2)}) %collective-permute-start.48) | collective-permute-done | bytes 262176 | tf_op jit(solution)/shard_map/ppermute | solution.py:20
  279.3 6.0 %collective-permute-done.59 = bf16[128,1024]{1,0:T(8,128)(2,1)} collective-permute-done((bf16[128,1024]{1,0:T(8,128)(2,1)}, bf16[128,1024]{1,0:T(8,128)(2,1)}, u32[]{:S(2)}, u32[]{:S(2)}) %collective-permute-start.59) | collective-permute-done | bytes 262176 | tf_op jit(solution)/shard_map/ppermute | solution.py:20
  286.6 5.1 %collective-permute-done.58 = bf16[128,1024]{1,0:T(8,128)(2,1)} collective-permute-done((bf16[128,1024]{1,0:T(8,128)(2,1)}, bf16[128,1024]{1,0:T(8,128)(2,1)}, u32[]{:S(2)}, u32[]{:S(2)}) %collective-permute-start.58) | collective-permute-done | bytes 262176 | tf_op jit(solution)/shard_map/ppermute | solution.py:20
  295.6 6.4 %collective-permute-done.55 = bf16[128,1024]{1,0:T(8,128)(2,1)} collective-permute-done((bf16[128,1024]{1,0:T(8,128)(2,1)}, bf16[128,1024]{1,0:T(8,128)(2,1)}, u32[]{:S(2)}, u32[]{:S(2)}) %collective-permute-start.55) | collective-permute-done | bytes 262176 | tf_op jit(solution)/shard_map/ppermute | solution.py:20
  318.3 12.7 %collective-permute-done.44 = bf16[128,1024]{1,0:T(8,128)(2,1)S(1)} collective-permute-done((bf16[128,1024]{1,0:T(8,128)(2,1)}, bf16[128,1024]{1,0:T(8,128)(2,1)S(1)}, u32[]{:S(2)}, u32[]{:S(2)}) %collective-permute-start.44) | collective-permute-done | bytes 262176 | tf_op jit(solution)/shard_map/ppermute | solution.py:20
  336.4 11.7 %reduce-scatter.2.cloned.1.call-done = f32[16,512]{1,0:T(8,128)} async-done(((f32[16,1024]{1,0:T(8,128)}), f32[16,512]{1,0:T(8,128)}) %reduce-scatter.2.cloned.1.call-update) | async-done | bytes 32784 | tf_op jit(solution)/shard_map/reduce_scatter | solution.py:165
  348.1 79.2 %psum.8 = f32[16,512]{1,0:T(8,128)} all-reduce(f32[16,512]{1,0:T(8,128)} %reduce-scatter.2.cloned.1.call-done), channel_id=1, replica_groups=mesh['context'=16,'fsdp'=2] {'context'}, use_global_device_ids=true, to_apply=%region_9.10 | all-reduce | flops 8192 | bytes 65536 | tf_op jit(solution)/shard_map/psum | solution.py:164
  (252 shorter events, 182.7 us)
Async XLA Ops:
  7.2 340.9 %reduce-scatter.2.cloned.1.call-start = ((), (), s32[]{:S(2)}) async-start(), calls=%async_computation.1 | async-start | bytes 98304 | tf_op jit(solution)/shard_map/reduce_scatter | solution.py:165
  7.2 21.7 %collective-permute-start.20 = (s32[1]{0:T(128)}, s32[1]{0:T(128)}, u32[]{:S(2)}, u32[]{:S(2)}) collective-permute-start(s32[1]{0:T(128)} %bitcast.10), channel_id=1, source_target_pairs={{0,2},{2,4},{4,6},{6,8},{8,10},{10,12},{12,14},{14,16},{16,18},{18... | collective-permute-start | bytes 20 | tf_op jit(solution)/shard_map/ppermute | solution.py:20
  17.2 40.2 %collective-permute-start = (bf16[128,1024]{0,1:T(8,128)(2,1)S(1)}, bf16[128,1024]{0,1:T(8,128)(2,1)S(1)}, u32[]{:S(2)}, u32[]{:S(2)}) collective-permute-start(bf16[128,1024]{0,1:T(8,128)(2,1)S(1)} %bitcast.304), channel_id=1, source_target_pairs={{0,2},{2,4},{4,6},{6,8},{8,10},{10,12},{12,14},{14,16},{16,18},{18... | collective-permute-start | bytes 786440 | tf_op jit(solution)/shard_map/ppermute | solution.py:20
  21.2 47.6 %collective-permute-start.30 = (bf16[128,1024]{0,1:T(8,128)(2,1)S(1)}, bf16[128,1024]{0,1:T(8,128)(2,1)S(1)}, u32[]{:S(2)}, u32[]{:S(2)}) collective-permute-start(bf16[128,1024]{0,1:T(8,128)(2,1)S(1)} %bitcast.302), channel_id=1, source_target_pairs={{0,2},{2,4},{4,6},{6,8},{8,10},{10,12},{12,14},{14,16},{16,18},{18... | collective-permute-start | bytes 786440 | tf_op jit(solution)/shard_map/ppermute | solution.py:20
  68.8 22.3 %collective-permute-start.31 = (bf16[128,1024]{0,1:T(8,128)(2,1)S(1)}, bf16[128,1024]{0,1:T(8,128)(2,1)S(1)}, u32[]{:S(2)}, u32[]{:S(2)}) collective-permute-start(bf16[128,1024]{0,1:T(8,128)(2,1)S(1)} %collective-permute-done.30), channel_id=1, source_target_pairs={{0,2},{2,4},{4,6},{6,8},{8,10},{10,12},{12,14},{14,16},{16,18},{18... | collective-permute-start | bytes 786440 | tf_op jit(solution)/shard_map/ppermute | solution.py:20
  72.5 20.8 %collective-permute-start.2 = (bf16[128,1024]{0,1:T(8,128)(2,1)S(1)}, bf16[128,1024]{0,1:T(8,128)(2,1)S(1)}, u32[]{:S(2)}, u32[]{:S(2)}) collective-permute-start(bf16[128,1024]{0,1:T(8,128)(2,1)S(1)} %collective-permute-done.1), channel_id=1, source_target_pairs={{0,2},{2,4},{4,6},{6,8},{8,10},{10,12},{12,14},{14,16},{16,18},{18... | collective-permute-start | bytes 786440 | tf_op jit(solution)/shard_map/ppermute | solution.py:20
  104.7 21.1 %collective-permute-start.33 = (bf16[128,1024]{0,1:T(8,128)(2,1)S(1)}, bf16[128,1024]{0,1:T(8,128)(2,1)S(1)}, u32[]{:S(2)}, u32[]{:S(2)}) collective-permute-start(bf16[128,1024]{0,1:T(8,128)(2,1)S(1)} %collective-permute-done.32), channel_id=1, source_target_pairs={{0,2},{2,4},{4,6},{6,8},{8,10},{10,12},{12,14},{14,16},{16,18},{18... | collective-permute-start | bytes 786440 | tf_op jit(solution)/shard_map/ppermute | solution.py:20
  108.8 19.2 %collective-permute-start.4 = (bf16[128,1024]{0,1:T(8,128)(2,1)S(1)}, bf16[128,1024]{0,1:T(8,128)(2,1)S(1)}, u32[]{:S(2)}, u32[]{:S(2)}) collective-permute-start(bf16[128,1024]{0,1:T(8,128)(2,1)S(1)} %collective-permute-done.3), channel_id=1, source_target_pairs={{0,2},{2,4},{4,6},{6,8},{8,10},{10,12},{12,14},{14,16},{16,18},{18... | collective-permute-start | bytes 786440 | tf_op jit(solution)/shard_map/ppermute | solution.py:20
  208.5 26.9 %collective-permute-start.49 = (bf16[128,1024]{1,0:T(8,128)(2,1)}, bf16[128,1024]{1,0:T(8,128)(2,1)}, u32[]{:S(2)}, u32[]{:S(2)}) collective-permute-start(bf16[128,1024]{1,0:T(8,128)(2,1)} %copy.97), channel_id=1, source_target_pairs={{20,0},{22,2},{24,4},{26,6},{28,8},{30,10},{21,1},{23,3},{25,5},{2... | collective-permute-start | bytes 786440 | tf_op jit(solution)/shard_map/ppermute | solution.py:20
  210.9 55.4 %collective-permute-start.48 = (bf16[128,1024]{1,0:T(8,128)(2,1)}, bf16[128,1024]{1,0:T(8,128)(2,1)}, u32[]{:S(2)}, u32[]{:S(2)}) collective-permute-start(bf16[128,1024]{1,0:T(8,128)(2,1)} %copy.96), channel_id=1, source_target_pairs={{18,0},{20,2},{22,4},{24,6},{26,8},{28,10},{30,12},{19,1},{21,3},{... | collective-permute-start | bytes 786440 | tf_op jit(solution)/shard_map/ppermute | solution.py:20
  213.0 58.4 %collective-permute-start.47 = (bf16[128,1024]{1,0:T(8,128)(2,1)}, bf16[128,1024]{1,0:T(8,128)(2,1)}, u32[]{:S(2)}, u32[]{:S(2)}) collective-permute-start(bf16[128,1024]{1,0:T(8,128)(2,1)} %copy.95), channel_id=1, source_target_pairs={{16,0},{18,2},{20,4},{22,6},{24,8},{26,10},{28,12},{30,14},{17,1},... | collective-permute-start | bytes 786440 | tf_op jit(solution)/shard_map/ppermute | solution.py:20
  215.1 57.5 %collective-permute-start.46 = (bf16[128,1024]{1,0:T(8,128)(2,1)}, bf16[128,1024]{1,0:T(8,128)(2,1)}, u32[]{:S(2)}, u32[]{:S(2)}) collective-permute-start(bf16[128,1024]{1,0:T(8,128)(2,1)} %copy.94), channel_id=1, source_target_pairs={{14,0},{16,2},{18,4},{20,6},{22,8},{24,10},{26,12},{28,14},{30,16}... | collective-permute-start | bytes 786440 | tf_op jit(solution)/shard_map/ppermute | solution.py:20
  219.4 54.6 %collective-permute-start.45 = (bf16[128,1024]{1,0:T(8,128)(2,1)}, bf16[128,1024]{1,0:T(8,128)(2,1)}, u32[]{:S(2)}, u32[]{:S(2)}) collective-permute-start(bf16[128,1024]{1,0:T(8,128)(2,1)} %copy.91), channel_id=1, source_target_pairs={{12,0},{14,2},{16,4},{18,6},{20,8},{22,10},{24,12},{26,14},{28,16}... | collective-permute-start | bytes 786440 | tf_op jit(solution)/shard_map/ppermute | solution.py:20
  235.4 49.9 %collective-permute-start.59 = (bf16[128,1024]{1,0:T(8,128)(2,1)}, bf16[128,1024]{1,0:T(8,128)(2,1)}, u32[]{:S(2)}, u32[]{:S(2)}) collective-permute-start(bf16[128,1024]{1,0:T(8,128)(2,1)} %copy.111), channel_id=1, source_target_pairs={{20,0},{22,2},{24,4},{26,6},{28,8},{30,10},{21,1},{23,3},{25,5},{2... | collective-permute-start | bytes 786440 | tf_op jit(solution)/shard_map/ppermute | solution.py:20
  266.2 25.5 %collective-permute-start.58 = (bf16[128,1024]{1,0:T(8,128)(2,1)}, bf16[128,1024]{1,0:T(8,128)(2,1)}, u32[]{:S(2)}, u32[]{:S(2)}) collective-permute-start(bf16[128,1024]{1,0:T(8,128)(2,1)} %copy.110), channel_id=1, source_target_pairs={{18,0},{20,2},{22,4},{24,6},{26,8},{28,10},{30,12},{19,1},{21,3},{... | collective-permute-start | bytes 786440 | tf_op jit(solution)/shard_map/ppermute | solution.py:20
  271.4 21.6 %collective-permute-start.57 = (bf16[128,1024]{1,0:T(8,128)(2,1)}, bf16[128,1024]{1,0:T(8,128)(2,1)}, u32[]{:S(2)}, u32[]{:S(2)}) collective-permute-start(bf16[128,1024]{1,0:T(8,128)(2,1)} %copy.109), channel_id=1, source_target_pairs={{16,0},{18,2},{20,4},{22,6},{24,8},{26,10},{28,12},{30,14},{17,1},... | collective-permute-start | bytes 786440 | tf_op jit(solution)/shard_map/ppermute | solution.py:20
  272.7 21.6 %collective-permute-start.56 = (bf16[128,1024]{1,0:T(8,128)(2,1)}, bf16[128,1024]{1,0:T(8,128)(2,1)}, u32[]{:S(2)}, u32[]{:S(2)}) collective-permute-start(bf16[128,1024]{1,0:T(8,128)(2,1)} %copy.108), channel_id=1, source_target_pairs={{14,0},{16,2},{18,4},{20,6},{22,8},{24,10},{26,12},{28,14},{30,16}... | collective-permute-start | bytes 786440 | tf_op jit(solution)/shard_map/ppermute | solution.py:20
  274.0 28.1 %collective-permute-start.55 = (bf16[128,1024]{1,0:T(8,128)(2,1)}, bf16[128,1024]{1,0:T(8,128)(2,1)}, u32[]{:S(2)}, u32[]{:S(2)}) collective-permute-start(bf16[128,1024]{1,0:T(8,128)(2,1)} %copy.106), channel_id=1, source_target_pairs={{12,0},{14,2},{16,4},{18,6},{20,8},{22,10},{24,12},{26,14},{28,16}... | collective-permute-start | bytes 786440 | tf_op jit(solution)/shard_map/ppermute | solution.py:20
  285.3 23.4 %collective-permute-start.54 = (bf16[128,1024]{1,0:T(8,128)(2,1)}, bf16[128,1024]{1,0:T(8,128)(2,1)}, u32[]{:S(2)}, u32[]{:S(2)}) collective-permute-start(bf16[128,1024]{1,0:T(8,128)(2,1)} %copy.105), channel_id=1, source_target_pairs={{10,0},{12,2},{14,4},{16,6},{18,8},{20,10},{22,12},{24,14},{26,16}... | collective-permute-start | bytes 786440 | tf_op jit(solution)/shard_map/ppermute | solution.py:20
  308.7 22.3 %collective-permute-start.44 = (bf16[128,1024]{1,0:T(8,128)(2,1)}, bf16[128,1024]{1,0:T(8,128)(2,1)S(1)}, u32[]{:S(2)}, u32[]{:S(2)}) collective-permute-start(bf16[128,1024]{1,0:T(8,128)(2,1)} %copy.90), channel_id=1, source_target_pairs={{10,0},{12,2},{14,4},{16,6},{18,8},{20,10},{22,12},{24,14},{26,16}... | collective-permute-start | bytes 786440 | tf_op jit(solution)/shard_map/ppermute | solution.py:20
  310.0 23.8 %collective-permute-start.43 = (bf16[128,1024]{1,0:T(8,128)(2,1)S(1)}, bf16[128,1024]{1,0:T(8,128)(2,1)S(1)}, u32[]{:S(2)}, u32[]{:S(2)}) collective-permute-start(bf16[128,1024]{1,0:T(8,128)(2,1)S(1)} %copy-done.16), channel_id=1, source_target_pairs={{8,0},{10,2},{12,4},{14,6},{16,8},{18,10},{20,12},{22,14},{24,16},... | collective-permute-start | bytes 786440 | tf_op jit(solution)/shard_map/ppermute | solution.py:20
  311.3 22.5 %collective-permute-start.42 = (bf16[128,1024]{1,0:T(8,128)(2,1)S(1)}, bf16[128,1024]{1,0:T(8,128)(2,1)S(1)}, u32[]{:S(2)}, u32[]{:S(2)}) collective-permute-start(bf16[128,1024]{1,0:T(8,128)(2,1)S(1)} %copy.88), channel_id=1, source_target_pairs={{6,0},{8,2},{10,4},{12,6},{14,8},{16,10},{18,12},{20,14},{22,16},{... | collective-permute-start | bytes 786440 | tf_op jit(solution)/shard_map/ppermute | solution.py:20
  312.7 21.2 %collective-permute-start.41 = (bf16[128,1024]{1,0:T(8,128)(2,1)S(1)}, bf16[128,1024]{1,0:T(8,128)(2,1)}, u32[]{:S(2)}, u32[]{:S(2)}) collective-permute-start(bf16[128,1024]{1,0:T(8,128)(2,1)S(1)} %copy.85), channel_id=1, source_target_pairs={{4,0},{6,2},{8,4},{10,6},{12,8},{14,10},{16,12},{18,14},{20,16},{2... | collective-permute-start | bytes 786440 | tf_op jit(solution)/shard_map/ppermute | solution.py:20
  314.0 19.8 %collective-permute-start.40 = (bf16[128,1024]{1,0:T(8,128)(2,1)S(1)}, bf16[128,1024]{1,0:T(8,128)(2,1)S(1)}, u32[]{:S(2)}, u32[]{:S(2)}) collective-permute-start(bf16[128,1024]{1,0:T(8,128)(2,1)S(1)} %copy.83), channel_id=1, source_target_pairs={{2,0},{4,2},{6,4},{8,6},{10,8},{12,10},{14,12},{16,14},{18,16},{20... | collective-permute-start | bytes 786440 | tf_op jit(solution)/shard_map/ppermute | solution.py:20
  (64 other events, 1543.1 us)
Sparse Core Ops, SparseCore 0:
  318.4 29.6 reduce-scatter.1
where the time goes:
time: 437 us; the launch traced here: 434 us
  starting transfers between devices  176 us (40%)
  waiting for transfers between devices  81.8 us (19%)
  blocking collectives  79.2 us (18%)
  local copies, waits for them, and re-layouts  32.6 us (7%)
  other arithmetic  25.3 us (6%)
  matrix products  22.4 us (5%)
  between operations  16.6 us (4%)
    ppermute x60, starting transfers between devices, shifted(): lax.ppermute(value, axis, [(source, source + steps) for source in range(i...  176 us
    psum x1, blocking collectives, local(): adapter_whole = lax.psum(adapter_term, 'context')  79.2 us
    ppermute x60, waiting for transfers between devices, shifted(): lax.ppermute(value, axis, [(source, source + steps) for source in range(i...  70.1 us
    slice x13, local copies, waits for them, and re-layouts, local(): value_terms[REACH - distance]  14.2 us
    reduce_scatter x1, waiting for transfers between devices, local(): lax.psum_scatter(adapter_whole, 'fsdp', scatter_dimension=1, tiled=True)  11.7 us
    slice x13, local copies, waits for them, and re-layouts, local(): key_terms[REACH - distance]  10.7 us
  transfers between devices with their start and end apart: 61, of which 15 were waited for; matrix products, arithmetic and copies ran while one was open for 14% of the time, Pallas kernels for 0%

commit v1 on v0

--- a/solution.py
+++ b/solution.py
@@ -1,6 +1,11 @@
+import functools
+import math
+
 import jax
 import jax.numpy as jnp
 from jax import lax
+from jax.experimental import pallas as pl
+from jax.experimental.pallas import tpu as pltpu
 from jax.sharding import PartitionSpec as P
 
 HQ = 16
@@ -8,6 +13,7 @@
 HEAD_SIZE = 128
 WINDOW = 1024
 REACH = 10
+ADAPTER_RANK = 16
 
 
 SCORE_SCALE = 168.0 ** (-0.5)
@@ -166,7 +172,367 @@
     return (grad_queries, grad_keys[None], value_gradient[None], adapter_grad)
 
 
+MESH = pl.DeviceIdType.MESH
+T = 128
+D = HEAD_SIZE
+EXP2_SCALE = SCORE_SCALE * math.log2(math.e)
+SIDE_ROWS = 24
+
+
+def lower_shard(block):
+    return max(0, 2 * block - REACH)
+
+
+def cols(index):
+    return pl.ds(pl.multiple_of(index * D, D), D)
+
+
+def head_kernel(
+    shards, side_ref, k_ref, v_ref, q_ref, do_ref,
+    dq_out, kv_out, ad_out,
+    sbuf, kbuf, vbuf, qbuf, dobuf, ktbuf, pbuf, acc, rx, fin, dqbuf, adpart, adbuf,
+    s_send, s_recv, k_send, k_recv, v_send, v_recv, q_send, q_recv, do_send, do_recv,
+    fk_send, fv_send, x_send, x_recv, dq_send, dq_recv, kv_send, kv_recv, ad_send, ad_recv,
+):
+    me = lax.axis_index("context")
+    core = lax.axis_index("fsdp")
+    other = 1 - core
+    row = me // KEY_VALUE_HEADS
+    head = me % KEY_VALUE_HEADS
+    blocks = shards // 2
+
+    def is_self(chip, dev):
+        return jnp.logical_and(chip == me, dev == core)
+
+    def remote(src, dst, ssem, rsem, chip, dev):
+        return pltpu.make_async_remote_copy(
+            src_ref=src, dst_ref=dst, send_sem=ssem, recv_sem=rsem,
+            device_id={"context": chip, "fsdp": dev}, device_id_type=MESH,
+        )
+
+    def send(src, dst, ssem, rsem, chip, dev):
+        mine = is_self(chip, dev)
+
+        @pl.when(mine)
+        def _():
+            pltpu.make_async_copy(src, dst, rsem).start()
+
+        @pl.when(jnp.logical_not(mine))
+        def _():
+            remote(src, dst, ssem, rsem, chip, dev).start()
+
+    def sent(src, dst, ssem, rsem, chip, dev):
+        @pl.when(jnp.logical_not(is_self(chip, dev)))
+        def _():
+            remote(src, dst, ssem, rsem, chip, dev).wait_send()
+
+    def arrived(dst, rsem):
+        pltpu.make_async_copy(dst, dst, rsem).wait()
+
+    barrier = pltpu.get_barrier_semaphore()
+
+    def greet(step, carry):
+        chip = lax.rem(me + step, shards)
+
+        @pl.when(step > 0)
+        def _():
+            pl.semaphore_signal(
+                barrier, inc=1, device_id={"context": chip, "fsdp": core}, device_id_type=MESH
+            )
+
+        pl.semaphore_signal(
+            barrier, inc=1, device_id={"context": chip, "fsdp": other}, device_id_type=MESH
+        )
+        return carry
+
+    lax.fori_loop(0, shards, greet, 0)
+    pl.semaphore_wait(barrier, 2 * shards - 1)
+
+    def target(step):
+        kv_head = lax.rem(step + me, KEY_VALUE_HEADS)
+        return kv_head, core * KEY_VALUE_HEADS + kv_head
+
+    def side_args(step, dev):
+        kv_head, chip = target(step)
+        return side_ref, sbuf.at[me], s_send.at[kv_head, dev], s_recv.at[me], chip, dev
+
+    def k_args(step):
+        kv_head, chip = target(step)
+        return k_ref.at[:, cols(kv_head)], kbuf.at[me], k_send.at[kv_head], k_recv.at[me], chip, me % 2
+
+    def v_args(step):
+        kv_head, chip = target(step)
+        return v_ref.at[:, cols(kv_head)], vbuf.at[me], v_send.at[kv_head], v_recv.at[me], chip, me % 2
+
+    def q_args(step, dev):
+        kv_head, chip = target(step)
+        return (q_ref.at[:, cols(2 * kv_head + dev)], qbuf.at[me], q_send.at[kv_head, dev],
+                q_recv.at[me], chip, dev)
+
+    def do_args(step, dev):
+        kv_head, chip = target(step)
+        return (do_ref.at[:, cols(2 * kv_head + dev)], dobuf.at[me], do_send.at[kv_head, dev],
+                do_recv.at[me], chip, dev)
+
+    def loop(count, body):
+        def step_fn(step, carry):
+            body(step)
+            return carry
+        lax.fori_loop(0, count, step_fn, 0)
+
+    def first(act):
+        def body(step):
+            act(*k_args(step))
+            act(*v_args(step))
+            act(*side_args(step, 0))
+            act(*side_args(step, 1))
+        return body
+
+    def second(act):
+        def body(step):
+            act(*q_args(step, 0))
+            act(*q_args(step, 1))
+        return body
+
+    def third(act):
+        def body(step):
+            act(*do_args(step, 0))
+            act(*do_args(step, 1))
+        return body
+
+    loop(KEY_VALUE_HEADS, first(send))
+    loop(KEY_VALUE_HEADS, second(send))
+    loop(KEY_VALUE_HEADS, third(send))
+
+    acc[...] = jnp.zeros_like(acc)
+
+    def forward(step):
+        shard = 2 * step + core
+        arrived(kbuf.at[shard], k_recv.at[shard])
+        remote(kbuf.at[shard], kbuf.at[shard], fk_send.at[shard], k_recv.at[shard], me, other).start()
+        arrived(vbuf.at[shard], v_recv.at[shard])
+        remote(vbuf.at[shard], vbuf.at[shard], fv_send.at[shard], v_recv.at[shard], me, other).start()
+
+    loop(blocks, forward)
+
+    def from_sibling(step):
+        shard = 2 * step + other
+        arrived(kbuf.at[shard], k_recv.at[shard])
+        arrived(vbuf.at[shard], v_recv.at[shard])
+
+    loop(blocks, from_sibling)
+
+    def side_in(step):
+        arrived(sbuf.at[step], s_recv.at[step])
+
+    loop(shards, side_in)
+
+    slot = lax.broadcasted_iota(jnp.int32, (T, 2 * T), 0).astype(jnp.float32)
+    lane = lax.broadcasted_iota(jnp.int32, (1, T), 1).astype(jnp.float32)
+    starts = []
+    total = 0
+    for block in range(blocks):
+        starts.append(total)
+        total += (2 * block + 2 - lower_shard(block)) * T
+
+    def dot(a, b, dims):
+        return lax.dot_general(a, b, (dims, ((), ())), preferred_element_type=jnp.float32)
+
+    for shard in range(shards):
+        ktbuf[:, shard * T : (shard + 1) * T] = kbuf[shard].T
+
+    for block in range(blocks):
+        low, high = lower_shard(block), 2 * block + 2
+        span = (high - low) * T
+        arrived(qbuf.at[2 * block], q_recv.at[2 * block])
+        arrived(qbuf.at[2 * block + 1], q_recv.at[2 * block + 1])
+        q = qbuf[2 * block : 2 * block + 2].reshape(2 * T, D)
+        k = kbuf[low:high].reshape(span, D)
+        raw = dot(k, q, ((1,), (1,)))
+        q_pos = jnp.concatenate(
+            [sbuf[2 * block, 17:18, :] + lane, sbuf[2 * block + 1, 17:18, :] + lane], axis=1
+        )
+        q_index = jnp.concatenate([lane, lane + T], axis=1)
+        pieces = []
+        for shard in range(low, high):
+            count = sbuf[shard, 16:17, :]
+            top = jnp.concatenate([count, count], axis=1) - 1.0
+            if shard >= 2 * block:
+                top = jnp.minimum(top, q_index - (shard - 2 * block) * T)
+            allowed = slot <= top
+            if (high - shard) * T > WINDOW:
+                offset = sbuf[shard, 17:18, :]
+                bottom = q_pos - jnp.concatenate([offset, offset], axis=1) - WINDOW
+                allowed = jnp.logical_and(allowed, slot > bottom)
+            piece = raw[(shard - low) * T : (shard - low + 1) * T] * EXP2_SCALE
+            pieces.append(jnp.where(allowed, piece, -1e30))
+        peak = pieces[0].max(axis=0, keepdims=True)
+        for piece in pieces[1:]:
+            peak = jnp.maximum(peak, piece.max(axis=0, keepdims=True))
+        weights = [jnp.exp2(piece - peak) for piece in pieces]
+        norm = weights[0].sum(axis=0, keepdims=True)
+        for weight in weights[1:]:
+            norm = norm + weight.sum(axis=0, keepdims=True)
+        inverse = 1.0 / norm
+        for number, weight in enumerate(weights):
+            begin = starts[block] + number * T
+            pbuf[begin : begin + T, :] = weight * inverse
+
+    def swap_args(block):
+        return (acc.at[other, pl.ds(2 * T * block, 2 * T)], rx.at[block], x_send.at[block],
+                x_recv.at[block], me, other)
+
+    def dq_args(shard):
+        return (dqbuf.at[shard], dq_out.at[:, cols(2 * head + core)], dq_send.at[shard],
+                dq_recv.at[2 * head + core], shard, row)
+
+    def kv_args(shard):
+        return (fin.at[shard], kv_out.at[core, :, cols(head)], kv_send.at[shard],
+                kv_recv.at[core, head], shard, row)
+
+    factor = jnp.where(core == 0, SCORE_SCALE, 1.0).astype(jnp.float32)
+    adapter = jnp.zeros((ADAPTER_RANK, D), jnp.float32)
+
+    def finish(block, adapter):
+        arrived(rx.at[block], x_recv.at[block])
+        whole = acc[core, pl.ds(2 * T * block, 2 * T), :] + rx[block]
+        half = (whole * factor).astype(jnp.bfloat16)
+        for part in range(2):
+            shard = 2 * block + part
+            fin[shard] = half[part * T : (part + 1) * T]
+            send(*kv_args(shard))
+            hidden = sbuf[shard, 0:ADAPTER_RANK, :].astype(jnp.bfloat16)
+            adapter = adapter + dot(hidden, half[part * T : (part + 1) * T], ((1,), (0,)))
+        return adapter
+
+    for block in reversed(range(blocks)):
+        low, high = lower_shard(block), 2 * block + 2
+        span = (high - low) * T
+        grads = []
+        for shard in (2 * block, 2 * block + 1):
+            arrived(dobuf.at[shard], do_recv.at[shard])
+            count = sbuf[shard, 16:17, :]
+            grads.append(jnp.where(slot[:, :D] < count, dobuf[shard].astype(jnp.float32), 0.0))
+        grad = jnp.concatenate(grads, axis=0).astype(jnp.bfloat16)
+        q = qbuf[2 * block : 2 * block + 2].reshape(2 * T, D)
+        v = vbuf[low:high].reshape(span, D)
+        probs = pbuf[starts[block] : starts[block] + span, :]
+        dprobs = dot(v, grad, ((1,), (1,)))
+        delta = jnp.sum(probs * dprobs, axis=0, keepdims=True)
+        dscores = (probs * (dprobs - delta)).astype(jnp.bfloat16)
+        dq = dot(ktbuf[:, low * T : high * T], dscores, ((1,), (0,))).T * SCORE_SCALE
+        dqbuf[2 * block] = dq[:T].astype(jnp.bfloat16)
+        dqbuf[2 * block + 1] = dq[T:].astype(jnp.bfloat16)
+        send(*dq_args(2 * block))
+        send(*dq_args(2 * block + 1))
+        acc[0, low * T : high * T, :] += dot(dscores, q, ((1,), (0,)))
+        acc[1, low * T : high * T, :] += dot(probs.astype(jnp.bfloat16), grad, ((1,), (0,)))
+        remote(*swap_args(block)).start()
+        if block + 1 < blocks:
+            adapter = finish(block + 1, adapter)
+    adapter = finish(0, adapter)
+    adpart[...] = adapter * ADAPTER_SCALE
+
+    half_heads = KEY_VALUE_HEADS // 2
+
+    def ad_args(step):
+        chip = lax.rem(me + step, shards)
+        return (adpart, adbuf.at[row, :, cols(head % half_heads)], ad_send.at[step],
+                ad_recv.at[row, head % half_heads], chip, head // half_heads)
+
+    @pl.when(core == 1)
+    def _():
+        loop(shards, lambda step: send(*ad_args(step)))
+
+    loop(KEY_VALUE_HEADS, first(sent))
+    loop(KEY_VALUE_HEADS, second(sent))
+    loop(KEY_VALUE_HEADS, third(sent))
+
+    def forward_sent(step):
+        shard = 2 * step + core
+        remote(kbuf.at[shard], kbuf.at[shard], fk_send.at[shard], k_recv.at[shard], me, other).wait_send()
+        remote(vbuf.at[shard], vbuf.at[shard], fv_send.at[shard], v_recv.at[shard], me, other).wait_send()
+
+    loop(blocks, forward_sent)
+    for block in range(blocks):
+        remote(*swap_args(block)).wait_send()
+    loop(shards, lambda shard: sent(*dq_args(shard)))
+    loop(shards, lambda shard: sent(*kv_args(shard)))
+
+    @pl.when(core == 1)
+    def _():
+        loop(shards, lambda step: sent(*ad_args(step)))
+
+    loop(HQ, lambda index: arrived(dq_out.at[:, cols(index)], dq_recv.at[index]))
+    for kind in range(2):
+        loop(KEY_VALUE_HEADS, lambda index: arrived(kv_out.at[kind, :, cols(index)], kv_recv.at[kind, index]))
+    for source in range(2):
+        for index in range(half_heads):
+            arrived(adbuf.at[source, :, index * D : (index + 1) * D], ad_recv.at[source, index])
+    ad_out[...] = adbuf[0] + adbuf[1]
+
+
+def by_head(shards, queries, keys, values, output_gradient, adapter_hidden, counts, offsets):
+    blocks = shards // 2
+    total = sum((2 * block + 2 - lower_shard(block)) * T for block in range(blocks))
+    side = jnp.concatenate(
+        [
+            adapter_hidden[0].astype(jnp.float32).T,
+            jnp.broadcast_to(counts.astype(jnp.float32), (1, T)),
+            jnp.broadcast_to(offsets.astype(jnp.float32), (1, T)),
+            jnp.zeros((SIDE_ROWS - ADAPTER_RANK - 2, T), jnp.float32),
+        ],
+        axis=0,
+    )
+    bf16, f32 = jnp.bfloat16, jnp.float32
+    dma = pltpu.SemaphoreType.DMA
+    anywhere = pl.BlockSpec(memory_space=pl.ANY)
+    vmem = pl.BlockSpec(memory_space=pltpu.VMEM)
+    dq, kv, adapter = pl.pallas_call(
+        functools.partial(head_kernel, shards),
+        out_shape=(
+            jax.ShapeDtypeStruct((T, HQ * D), bf16),
+            jax.ShapeDtypeStruct((2, T, KEY_VALUE_HEADS * D), bf16),
+            jax.ShapeDtypeStruct((ADAPTER_RANK, KEY_VALUE_HEADS * D // 2), f32),
+        ),
+        in_specs=[anywhere] * 5,
+        out_specs=(anywhere, anywhere, vmem),
+        scratch_shapes=[
+            pltpu.VMEM((shards, SIDE_ROWS, T), f32),
+            pltpu.VMEM((shards, T, D), bf16),
+            pltpu.VMEM((shards, T, D), bf16),
+            pltpu.VMEM((shards, T, D), bf16),
+            pltpu.VMEM((shards, T, D), bf16),
+            pltpu.VMEM((D, shards * T), bf16),
+            pltpu.VMEM((total, 2 * T), f32),
+            pltpu.VMEM((2, shards * T, D), f32),
+            pltpu.VMEM((blocks, 2 * T, D), f32),
+            pltpu.VMEM((shards, T, D), bf16),
+            pltpu.VMEM((shards, T, D), bf16),
+            pltpu.VMEM((ADAPTER_RANK, D), f32),
+            pltpu.VMEM((2, ADAPTER_RANK, KEY_VALUE_HEADS * D // 2), f32),
+            dma((KEY_VALUE_HEADS, 2)), dma((shards,)),
+            dma((KEY_VALUE_HEADS,)), dma((shards,)),
+            dma((KEY_VALUE_HEADS,)), dma((shards,)),
+            dma((KEY_VALUE_HEADS, 2)), dma((shards,)),
+            dma((KEY_VALUE_HEADS, 2)), dma((shards,)),
+            dma((shards,)), dma((shards,)),
+            dma((blocks,)), dma((blocks,)),
+            dma((shards,)), dma((HQ,)),
+            dma((shards,)), dma((2, KEY_VALUE_HEADS)),
+            dma((shards,)), dma((2, KEY_VALUE_HEADS // 2)),
+        ],
+        compiler_params=pltpu.CompilerParams(
+            collective_id=0, has_side_effects=True, vmem_limit_bytes=48 * 1024 * 1024
+        ),
+    )(side, keys[0], values[0], queries[0], output_gradient[0])
+    return dq[None], kv[0][None], kv[1][None], adapter
+
+
 def solution(mesh):
+    shards = mesh.shape["context"]
+    fits = shards == 2 * KEY_VALUE_HEADS and mesh.shape["fsdp"] == 2
+    body = functools.partial(by_head, shards) if fits else local
     in_specs = (
         P("fsdp", "context", None),
         P("fsdp", "context", None),
@@ -182,4 +548,4 @@
         P("fsdp", "context", None),
         P(None, "fsdp"),
     )
-    return jax.shard_map(local, mesh=mesh, in_specs=in_specs, out_specs=out_specs, check_vma=False)
+    return jax.shard_map(body, mesh=mesh, in_specs=in_specs, out_specs=out_specs, check_vma=False)

time: 437 us -> 91.9 us (0.21)
  starting transfers between devices: 176 us -> 0 us
  Pallas kernels: 0 us -> 82.5 us
  waiting for transfers between devices: 81.8 us -> 0 us
  blocking collectives: 79.2 us -> 0 us
  local copies, waits for them, and re-layouts: 32.6 us -> 7.05 us
  other arithmetic: 25.3 us -> 0.08 us
  matrix products: 22.4 us -> 0 us
  between operations: 16.6 us -> 1.95 us
    ppermute x60 -> x0, starting transfers between devices: 176 us -> none  [shifted(): lax.ppermute(value, axis, [(source, source + steps) for source in range(i...]
    pallas_call x0 -> x1, Pallas kernels: none -> 82.5 us  [by_head(): pl.pallas_call(functools.partial(head_kernel, shards), out_shape=(jax.Sha...]
    psum x1 -> x0, blocking collectives: 79.2 us -> none  [local(): adapter_whole = lax.psum(adapter_term, 'context')]
    ppermute x60 -> x0, waiting for transfers between devices: 70.1 us -> none  [shifted(): lax.ppermute(value, axis, [(source, source + steps) for source in range(i...]
    slice x26 -> x1, local copies, waits for them, and re-layouts: 24.9 us -> 0.82 us  [by_head(): return (dq[None], kv[0][None], kv[1][None], adapter)]
    dot_general x16 -> x0, matrix products: 22.4 us -> none  [the longest x3 6.4 us: local(): jnp.einsum('gjtk,kgd->tgjd', dscores, second_key_piece, preferred_element...]
    reduce_scatter x1 -> x0, waiting for transfers between devices: 11.7 us -> none  [local(): lax.psum_scatter(adapter_whole, 'fsdp', scatter_dimension=1, tiled=True)]
    add x13 -> x0, other arithmetic: 6.4 us -> none  [the longest x10 6.35 us: local(): shard_data[2][0] + slot_ids]
  transfers between devices with their start and end apart: 61 -> 0, of which waited for: 15 -> 0; matrix products, arithmetic and copies ran while one was open for 14% -> 0% of each run, Pallas kernels for 0% -> 0%
where the time goes in v1:
time: 91.9 us; the launch traced here: 91.6 us
  Pallas kernels  82.5 us (90%)
  local copies, waits for them, and re-layouts  7.05 us (8%)
  between operations  1.95 us (2%)
    pallas_call x1, Pallas kernels, by_head(): pl.pallas_call(functools.partial(head_kernel, shards), out_shape=(jax.Sha...  82.5 us
    unnamed x12, local copies, waits for them, and re-layouts  5.99 us

profile of v1, /device:TPU:0, one launch (start us, length us, event | category | flops | bytes accessed | tf_op | source)
XLA Modules:
  0.0 91.6 jit_solution(9031171183598755280)
XLA Ops:
  1.9 0.1 pad.1.clone
  2.0 0.1 pad.2.clone
  2.1 0.0 copy-start.4
  2.1 0.1 pad.3.clone
  2.2 0.6 copy-done.4
  2.8 0.1 maximum_maximum_fusion.side_ref
  2.8 0.0 copy-start
  2.8 1.0 %copy-done = bf16[1,128,2048]{2,1,0:T(8,128)(2,1)S(1)} copy-done((bf16[1,128,2048]{2,1,0:T(8,128)(2,1)S(1)}, bf16[1,128,2048]{2,1,0:T(8,128)(2,1)}, u32[]{:S(2)}) %copy-start) | copy-done | bytes 524312
  3.9 0.0 copy-start.1
  3.9 1.0 %copy-done.1 = bf16[1,128,2048]{2,1,0:T(8,128)(2,1)S(1)} copy-done((bf16[1,128,2048]{2,1,0:T(8,128)(2,1)S(1)}, bf16[1,128,2048]{2,1,0:T(8,128)(2,1)}, u32[]{:S(2)}) %copy-start.1) | copy-done | bytes 524312
  4.9 0.0 copy-start.2
  4.9 0.9 %copy-done.2 = bf16[1,128,1024]{2,1,0:T(8,128)(2,1)S(1)} copy-done((bf16[1,128,1024]{2,1,0:T(8,128)(2,1)S(1)}, bf16[1,128,1024]{2,1,0:T(8,128)(2,1)}, u32[]{:S(2)}) %copy-start.2) | copy-done | bytes 262168
  5.9 0.0 copy-start.3
  5.9 0.9 %copy-done.3 = bf16[1,128,1024]{2,1,0:T(8,128)(2,1)S(1)} copy-done((bf16[1,128,1024]{2,1,0:T(8,128)(2,1)S(1)}, bf16[1,128,1024]{2,1,0:T(8,128)(2,1)}, u32[]{:S(2)}) %copy-start.3) | copy-done | bytes 262168
  6.8 82.5 %shard_map.102 = (bf16[128,2048]{1,0:T(8,128)(2,1)S(1)}, bf16[2,128,1024]{2,1,0:T(8,128)(2,1)S(1)}, f32[16,512]{1,0:T(8,128)S(1)}) custom-call(f32[24,128]{1,0:T(8,128)S(1)} %maximum_maximum_fusion.side_ref, bf16[128,1024]{1,0:T(8,128)(2,1)S(1)} %bitcast.19, bf16[128,1024]{1,0:T(8,128)(2,1)S(1)} %bitcast.20, bf16[128,2048]{1,0:T(8,128)(2,1)S(1)} %bitcast.16, ...), custom_call_target="tpu_custom_call" | custom-call | tf_op jit(solution)/shard_map/pallas_call | solution.py:491
  89.3 0.8 fusion
  90.1 0.8 copy.15
  90.9 0.6 copy.16
  (2 shorter events, 0.0 us)
Async XLA Ops:
  2.1 0.7 copy-start.4
  2.8 1.0 %copy-start = (bf16[1,128,2048]{2,1,0:T(8,128)(2,1)S(1)}, bf16[1,128,2048]{2,1,0:T(8,128)(2,1)}, u32[]{:S(2)}) copy-start(bf16[1,128,2048]{2,1,0:T(8,128)(2,1)} %param.7) | copy-start | bytes 1572868
  3.9 1.0 %copy-start.1 = (bf16[1,128,2048]{2,1,0:T(8,128)(2,1)S(1)}, bf16[1,128,2048]{2,1,0:T(8,128)(2,1)}, u32[]{:S(2)}) copy-start(bf16[1,128,2048]{2,1,0:T(8,128)(2,1)} %param.10) | copy-start | bytes 1572868
  4.9 0.9 %copy-start.2 = (bf16[1,128,1024]{2,1,0:T(8,128)(2,1)S(1)}, bf16[1,128,1024]{2,1,0:T(8,128)(2,1)}, u32[]{:S(2)}) copy-start(bf16[1,128,1024]{2,1,0:T(8,128)(2,1)} %param.8) | copy-start | bytes 786436
  5.9 0.9 %copy-start.3 = (bf16[1,128,1024]{2,1,0:T(8,128)(2,1)S(1)}, bf16[1,128,1024]{2,1,0:T(8,128)(2,1)}, u32[]{:S(2)}) copy-start(bf16[1,128,1024]{2,1,0:T(8,128)(2,1)} %param.9) | copy-start | bytes 786436

commit v2 on v1

--- a/solution.py
+++ b/solution.py
@@ -176,7 +176,6 @@
 T = 128
 D = HEAD_SIZE
 EXP2_SCALE = SCORE_SCALE * math.log2(math.e)
-SIDE_ROWS = 24
 
 
 def lower_shard(block):
@@ -188,10 +187,10 @@
 
 
 def head_kernel(
-    shards, side_ref, k_ref, v_ref, q_ref, do_ref,
-    dq_out, kv_out, ad_out,
-    sbuf, kbuf, vbuf, qbuf, dobuf, ktbuf, pbuf, acc, rx, fin, dqbuf, adpart, adbuf,
-    s_send, s_recv, k_send, k_recv, v_send, v_recv, q_send, q_recv, do_send, do_recv,
+    shards, count_ref, offset_ref, hidden_ref, k_ref, v_ref, q_ref, do_ref,
+    dq_out, dk_out, dv_out, ad_out,
+    side, sbuf, hbuf, kbuf, vbuf, qbuf, dobuf, ktbuf, pbuf, acc, rx, fin, dqbuf, adpart, adbuf,
+    s_send, s_recv, h_send, h_recv, k_send, k_recv, v_send, v_recv, q_send, q_recv, do_send, do_recv,
     fk_send, fv_send, x_send, x_recv, dq_send, dq_recv, kv_send, kv_recv, ad_send, ad_recv,
 ):
     me = lax.axis_index("context")
@@ -246,15 +245,23 @@
         return carry
 
     lax.fori_loop(0, shards, greet, 0)
+    side[0:1, :] = jnp.full((1, T), count_ref[0, 0].astype(jnp.float32))
+    side[1:2, :] = jnp.full((1, T), offset_ref[0, 0].astype(jnp.float32))
+    acc[...] = jnp.zeros_like(acc)
+    adpart[...] = jnp.zeros_like(adpart)
     pl.semaphore_wait(barrier, 2 * shards - 1)
 
     def target(step):
-        kv_head = lax.rem(step + me, KEY_VALUE_HEADS)
+        kv_head = jnp.bitwise_xor(step, head)
         return kv_head, core * KEY_VALUE_HEADS + kv_head
 
     def side_args(step, dev):
         kv_head, chip = target(step)
-        return side_ref, sbuf.at[me], s_send.at[kv_head, dev], s_recv.at[me], chip, dev
+        return side, sbuf.at[me], s_send.at[kv_head, dev], s_recv.at[me], chip, dev
+
+    def hidden_args(step):
+        kv_head, chip = target(step)
+        return hidden_ref, hbuf.at[me], h_send.at[kv_head], h_recv.at[me], chip, 1
 
     def k_args(step):
         kv_head, chip = target(step)
@@ -298,13 +305,12 @@
         def body(step):
             act(*do_args(step, 0))
             act(*do_args(step, 1))
+            act(*hidden_args(step))
         return body
 
     loop(KEY_VALUE_HEADS, first(send))
     loop(KEY_VALUE_HEADS, second(send))
     loop(KEY_VALUE_HEADS, third(send))
-
-    acc[...] = jnp.zeros_like(acc)
 
     def forward(step):
         shard = 2 * step + core
@@ -350,18 +356,18 @@
         k = kbuf[low:high].reshape(span, D)
         raw = dot(k, q, ((1,), (1,)))
         q_pos = jnp.concatenate(
-            [sbuf[2 * block, 17:18, :] + lane, sbuf[2 * block + 1, 17:18, :] + lane], axis=1
+            [sbuf[2 * block, 1:2, :] + lane, sbuf[2 * block + 1, 1:2, :] + lane], axis=1
         )
         q_index = jnp.concatenate([lane, lane + T], axis=1)
         pieces = []
         for shard in range(low, high):
-            count = sbuf[shard, 16:17, :]
+            count = sbuf[shard, 0:1, :]
             top = jnp.concatenate([count, count], axis=1) - 1.0
             if shard >= 2 * block:
                 top = jnp.minimum(top, q_index - (shard - 2 * block) * T)
             allowed = slot <= top
             if (high - shard) * T > WINDOW:
-                offset = sbuf[shard, 17:18, :]
+                offset = sbuf[shard, 1:2, :]
                 bottom = q_pos - jnp.concatenate([offset, offset], axis=1) - WINDOW
                 allowed = jnp.logical_and(allowed, slot > bottom)
             piece = raw[(shard - low) * T : (shard - low + 1) * T] * EXP2_SCALE
@@ -386,32 +392,44 @@
         return (dqbuf.at[shard], dq_out.at[:, cols(2 * head + core)], dq_send.at[shard],
                 dq_recv.at[2 * head + core], shard, row)
 
-    def kv_args(shard):
-        return (fin.at[shard], kv_out.at[core, :, cols(head)], kv_send.at[shard],
-                kv_recv.at[core, head], shard, row)
+    def kv_args(shard, out, kind):
+        return (fin.at[shard], out.at[:, cols(head)], kv_send.at[shard],
+                kv_recv.at[kind, head], shard, row)
+
+    def kv_each(shard, act):
+        @pl.when(core == 0)
+        def _():
+            act(*kv_args(shard, dk_out, 0))
+
+        @pl.when(core == 1)
+        def _():
+            act(*kv_args(shard, dv_out, 1))
 
     factor = jnp.where(core == 0, SCORE_SCALE, 1.0).astype(jnp.float32)
-    adapter = jnp.zeros((ADAPTER_RANK, D), jnp.float32)
-
-    def finish(block, adapter):
-        arrived(rx.at[block], x_recv.at[block])
-        whole = acc[core, pl.ds(2 * T * block, 2 * T), :] + rx[block]
-        half = (whole * factor).astype(jnp.bfloat16)
-        for part in range(2):
-            shard = 2 * block + part
-            fin[shard] = half[part * T : (part + 1) * T]
-            send(*kv_args(shard))
-            hidden = sbuf[shard, 0:ADAPTER_RANK, :].astype(jnp.bfloat16)
-            adapter = adapter + dot(hidden, half[part * T : (part + 1) * T], ((1,), (0,)))
-        return adapter
-
-    for block in reversed(range(blocks)):
+
+    def turned(base, step):
+        return base + jnp.bitwise_xor(step, lax.rem(me, 4))
+
+    def finish(pair):
+        for block in (2 * pair, 2 * pair + 1):
+            arrived(rx.at[block], x_recv.at[block])
+            whole = acc[core, pl.ds(2 * T * block, 2 * T), :] + rx[block]
+            half = (whole * factor).astype(jnp.bfloat16)
+            fin[2 * block] = half[:T]
+            fin[2 * block + 1] = half[T:]
+        loop(4, lambda step: kv_each(turned(4 * pair, step), send))
+
+    def swap(pair):
+        remote(*swap_args(2 * pair)).start()
+        remote(*swap_args(2 * pair + 1)).start()
+
+    def block_grads(block):
         low, high = lower_shard(block), 2 * block + 2
         span = (high - low) * T
         grads = []
         for shard in (2 * block, 2 * block + 1):
             arrived(dobuf.at[shard], do_recv.at[shard])
-            count = sbuf[shard, 16:17, :]
+            count = sbuf[shard, 0:1, :]
             grads.append(jnp.where(slot[:, :D] < count, dobuf[shard].astype(jnp.float32), 0.0))
         grad = jnp.concatenate(grads, axis=0).astype(jnp.bfloat16)
         q = qbuf[2 * block : 2 * block + 2].reshape(2 * T, D)
@@ -423,15 +441,33 @@
         dq = dot(ktbuf[:, low * T : high * T], dscores, ((1,), (0,))).T * SCORE_SCALE
         dqbuf[2 * block] = dq[:T].astype(jnp.bfloat16)
         dqbuf[2 * block + 1] = dq[T:].astype(jnp.bfloat16)
-        send(*dq_args(2 * block))
-        send(*dq_args(2 * block + 1))
         acc[0, low * T : high * T, :] += dot(dscores, q, ((1,), (0,)))
         acc[1, low * T : high * T, :] += dot(probs.astype(jnp.bfloat16), grad, ((1,), (0,)))
-        remote(*swap_args(block)).start()
-        if block + 1 < blocks:
-            adapter = finish(block + 1, adapter)
-    adapter = finish(0, adapter)
-    adpart[...] = adapter * ADAPTER_SCALE
+
+    pairs = blocks // 2
+
+    def pair_grads(pair, order):
+        for block in order:
+            block_grads(2 * pair + block)
+        loop(4, lambda step: send(*dq_args(turned(4 * pair, step))))
+
+    @pl.when(row == 0)
+    def _():
+        for pair in reversed(range(pairs)):
+            pair_grads(pair, (1, 0))
+            swap(pair)
+            if pair + 1 < pairs:
+                finish(pair + 1)
+        finish(0)
+
+    @pl.when(row == 1)
+    def _():
+        for pair in range(pairs):
+            pair_grads(pair, (0, 1))
+        for pair in range(pairs):
+            swap(pair)
+        for pair in range(pairs):
+            finish(pair)
 
     half_heads = KEY_VALUE_HEADS // 2
 
@@ -442,6 +478,10 @@
 
     @pl.when(core == 1)
     def _():
+        for shard in range(shards):
+            arrived(hbuf.at[shard], h_recv.at[shard])
+            adpart[...] += dot(hbuf[shard], fin[shard], ((1,), (0,)))
+        adpart[...] *= ADAPTER_SCALE
         loop(shards, lambda step: send(*ad_args(step)))
 
     loop(KEY_VALUE_HEADS, first(sent))
@@ -457,15 +497,15 @@
     for block in range(blocks):
         remote(*swap_args(block)).wait_send()
     loop(shards, lambda shard: sent(*dq_args(shard)))
-    loop(shards, lambda shard: sent(*kv_args(shard)))
+    loop(shards, lambda shard: kv_each(shard, sent))
 
     @pl.when(core == 1)
     def _():
         loop(shards, lambda step: sent(*ad_args(step)))
 
     loop(HQ, lambda index: arrived(dq_out.at[:, cols(index)], dq_recv.at[index]))
-    for kind in range(2):
-        loop(KEY_VALUE_HEADS, lambda index: arrived(kv_out.at[kind, :, cols(index)], kv_recv.at[kind, index]))
+    loop(KEY_VALUE_HEADS, lambda index: arrived(dk_out.at[:, cols(index)], kv_recv.at[0, index]))
+    loop(KEY_VALUE_HEADS, lambda index: arrived(dv_out.at[:, cols(index)], kv_recv.at[1, index]))
     for source in range(2):
         for index in range(half_heads):
             arrived(adbuf.at[source, :, index * D : (index + 1) * D], ad_recv.at[source, index])
@@ -475,30 +515,25 @@
 def by_head(shards, queries, keys, values, output_gradient, adapter_hidden, counts, offsets):
     blocks = shards // 2
     total = sum((2 * block + 2 - lower_shard(block)) * T for block in range(blocks))
-    side = jnp.concatenate(
-        [
-            adapter_hidden[0].astype(jnp.float32).T,
-            jnp.broadcast_to(counts.astype(jnp.float32), (1, T)),
-            jnp.broadcast_to(offsets.astype(jnp.float32), (1, T)),
-            jnp.zeros((SIDE_ROWS - ADAPTER_RANK - 2, T), jnp.float32),
-        ],
-        axis=0,
-    )
     bf16, f32 = jnp.bfloat16, jnp.float32
     dma = pltpu.SemaphoreType.DMA
     anywhere = pl.BlockSpec(memory_space=pl.ANY)
     vmem = pl.BlockSpec(memory_space=pltpu.VMEM)
-    dq, kv, adapter = pl.pallas_call(
+    scalar = pl.BlockSpec(memory_space=pltpu.SMEM)
+    dq, dk, dv, adapter = pl.pallas_call(
         functools.partial(head_kernel, shards),
         out_shape=(
             jax.ShapeDtypeStruct((T, HQ * D), bf16),
-            jax.ShapeDtypeStruct((2, T, KEY_VALUE_HEADS * D), bf16),
+            jax.ShapeDtypeStruct((T, KEY_VALUE_HEADS * D), bf16),
+            jax.ShapeDtypeStruct((T, KEY_VALUE_HEADS * D), bf16),
             jax.ShapeDtypeStruct((ADAPTER_RANK, KEY_VALUE_HEADS * D // 2), f32),
         ),
-        in_specs=[anywhere] * 5,
-        out_specs=(anywhere, anywhere, vmem),
+        in_specs=[scalar] * 2 + [anywhere] * 5,
+        out_specs=(anywhere, anywhere, anywhere, vmem),
         scratch_shapes=[
-            pltpu.VMEM((shards, SIDE_ROWS, T), f32),
+            pltpu.VMEM((2, T), f32),
+            pltpu.VMEM((shards, 2, T), f32),
+            pltpu.VMEM((shards, ADAPTER_RANK, T), bf16),
             pltpu.VMEM((shards, T, D), bf16),
             pltpu.VMEM((shards, T, D), bf16),
             pltpu.VMEM((shards, T, D), bf16),
@@ -514,6 +549,7 @@
             dma((KEY_VALUE_HEADS, 2)), dma((shards,)),
             dma((KEY_VALUE_HEADS,)), dma((shards,)),
             dma((KEY_VALUE_HEADS,)), dma((shards,)),
+            dma((KEY_VALUE_HEADS,)), dma((shards,)),
             dma((KEY_VALUE_HEADS, 2)), dma((shards,)),
             dma((KEY_VALUE_HEADS, 2)), dma((shards,)),
             dma((shards,)), dma((shards,)),
@@ -523,10 +559,10 @@
             dma((shards,)), dma((2, KEY_VALUE_HEADS // 2)),
         ],
         compiler_params=pltpu.CompilerParams(
-            collective_id=0, has_side_effects=True, vmem_limit_bytes=48 * 1024 * 1024
+            collective_id=0, has_side_effects=True, vmem_limit_bytes=63 * 1024 * 1024
         ),
-    )(side, keys[0], values[0], queries[0], output_gradient[0])
-    return dq[None], kv[0][None], kv[1][None], adapter
+    )(counts, offsets, adapter_hidden[0].T, keys[0], values[0], queries[0], output_gradient[0])
+    return dq[None], dk[None], dv[None], adapter
 
 
 def solution(mesh):

time: 91.9 us -> 79.1 us (0.86)
  Pallas kernels: 82.5 us -> 72.5 us
  local copies, waits for them, and re-layouts: 7.05 us -> 4.34 us
    pallas_call x1, Pallas kernels: 82.5 us -> 72.5 us  [by_head(): pl.pallas_call(functools.partial(head_kernel, shards), out_shape=(jax.Sha...]
    unnamed x12 -> x10, local copies, waits for them, and re-layouts: 5.99 us -> 4.34 us
where the time goes in v2:
time: 79.1 us; the launch traced here: 78.8 us
  Pallas kernels  72.5 us (92%)
  local copies, waits for them, and re-layouts  4.34 us (5%)
  between operations  1.94 us (2%)
    pallas_call x1, Pallas kernels, by_head(): pl.pallas_call(functools.partial(head_kernel, shards), out_shape=(jax.Sha...  72.5 us
    unnamed x10, local copies, waits for them, and re-layouts  4.34 us

profile of v2, /device:TPU:0, one launch (start us, length us, event | category | flops | bytes accessed | tf_op | source)
XLA Modules:
  0.0 78.8 jit_solution(5636491548644346563)
XLA Ops:
  1.9 72.5 %shard_map.102 = (bf16[128,2048]{1,0:T(8,128)(2,1)}, bf16[128,1024]{1,0:T(8,128)(2,1)}, bf16[128,1024]{1,0:T(8,128)(2,1)}, f32[16,512]{1,0:T(8,128)}) custom-call(s32[1,1]{1,0:T(1,128)S(6)} %copy.15.count_ref, s32[1,1]{1,0:T(1,128)S(6)} %copy.16.offset_ref, bf16[16,128]{1,0:T(8,128)(2,1)} %bitcast.17, bf16[128,1024]{1,0:T(8,128)(2,1)} %bitcast.15, ...), custom_call_target="tpu_custom_call" | custom-call | tf_op jit(solution)/shard_map/pallas_call | solution.py:523
  74.5 0.0 copy-start.1
  74.5 1.9 %copy.17 = bf16[1,128,2048]{2,1,0:T(8,128)(2,1)} copy(bf16[1,128,2048]{2,1,0:T(8,128)(2,1)} %bitcast.10) | data formatting | bytes 1048576
  76.4 0.0 copy-done.1
  76.4 0.0 copy-start
  76.4 0.7 copy.18
  77.1 0.3 copy-done
  77.4 0.0 copy-start.2
  77.4 0.7 copy.19
  78.1 0.1 copy-done.2
  78.2 0.6 copy.20
Async XLA Ops:
  74.5 1.9 %copy-start.1 = (bf16[128,1024]{1,0:T(8,128)(2,1)S(1)}, bf16[128,1024]{1,0:T(8,128)(2,1)}, u32[]{:S(2)}) copy-start(bf16[128,1024]{1,0:T(8,128)(2,1)} %get-tuple-element.9) | copy-start | bytes 786436
  76.4 1.0 %copy-start = (bf16[128,1024]{1,0:T(8,128)(2,1)S(1)}, bf16[128,1024]{1,0:T(8,128)(2,1)}, u32[]{:S(2)}) copy-start(bf16[128,1024]{1,0:T(8,128)(2,1)} %get-tuple-element.10) | copy-start | bytes 786436
  77.4 0.8 copy-start.2

commit v3 on v2

--- a/solution.py
+++ b/solution.py
@@ -188,8 +188,8 @@
 
 def head_kernel(
     shards, count_ref, offset_ref, hidden_ref, k_ref, v_ref, q_ref, do_ref,
-    dq_out, dk_out, dv_out, ad_out,
-    side, sbuf, hbuf, kbuf, vbuf, qbuf, dobuf, ktbuf, pbuf, acc, rx, fin, dqbuf, adpart, adbuf,
+    dq_out, dk_out, dv_out, adbuf,
+    side, sbuf, hbuf, kbuf, vbuf, qbuf, dobuf, ktbuf, pbuf, acc, rx, fin, dqbuf, adpart,
     s_send, s_recv, h_send, h_recv, k_send, k_recv, v_send, v_recv, q_send, q_recv, do_send, do_recv,
     fk_send, fv_send, x_send, x_recv, dq_send, dq_recv, kv_send, kv_recv, ad_send, ad_recv,
 ):
@@ -509,7 +509,40 @@
     for source in range(2):
         for index in range(half_heads):
             arrived(adbuf.at[source, :, index * D : (index + 1) * D], ad_recv.at[source, index])
-    ad_out[...] = adbuf[0] + adbuf[1]
+
+
+def settle_kernel(dq, dk, dv, adapters, dq_out, dk_out, dv_out, ad_out, dq_held, dk_held, dv_held, in_sems, out_sems):
+    part = T // 4
+    copies = []
+    for index, (src, held, dst) in enumerate(
+        ((dq, dq_held, dq_out), (dk, dk_held, dk_out), (dv, dv_held, dv_out))
+    ):
+        for step in range(4):
+            rows = pl.ds(step * part, part)
+            first = pltpu.make_async_copy(src.at[rows], held.at[rows], in_sems.at[index, step])
+            second = pltpu.make_async_copy(held.at[rows], dst.at[0, rows], out_sems.at[index, step])
+            first.start()
+            copies.append((first, second))
+    ad_out[...] = adapters[0] + adapters[1]
+    for first, second in copies:
+        first.wait()
+        second.start()
+    for first, second in copies:
+        second.wait()
+
+
+def settle(dq, dk, dv, adapters):
+    anywhere = pl.BlockSpec(memory_space=pl.ANY)
+    vmem = pl.BlockSpec(memory_space=pltpu.VMEM)
+    return pl.pallas_call(
+        settle_kernel,
+        out_shape=tuple(jax.ShapeDtypeStruct((1,) + grad.shape, grad.dtype) for grad in (dq, dk, dv))
+        + (jax.ShapeDtypeStruct(adapters.shape[1:], adapters.dtype),),
+        in_specs=[anywhere] * 3 + [vmem],
+        out_specs=(anywhere,) * 3 + (vmem,),
+        scratch_shapes=[pltpu.VMEM(grad.shape, grad.dtype) for grad in (dq, dk, dv)]
+        + [pltpu.SemaphoreType.DMA((3, 4))] * 2,
+    )(dq, dk, dv, adapters)
 
 
 def by_head(shards, queries, keys, values, output_gradient, adapter_hidden, counts, offsets):
@@ -526,7 +559,7 @@
             jax.ShapeDtypeStruct((T, HQ * D), bf16),
             jax.ShapeDtypeStruct((T, KEY_VALUE_HEADS * D), bf16),
             jax.ShapeDtypeStruct((T, KEY_VALUE_HEADS * D), bf16),
-            jax.ShapeDtypeStruct((ADAPTER_RANK, KEY_VALUE_HEADS * D // 2), f32),
+            jax.ShapeDtypeStruct((2, ADAPTER_RANK, KEY_VALUE_HEADS * D // 2), f32),
         ),
         in_specs=[scalar] * 2 + [anywhere] * 5,
         out_specs=(anywhere, anywhere, anywhere, vmem),
@@ -545,7 +578,6 @@
             pltpu.VMEM((shards, T, D), bf16),
             pltpu.VMEM((shards, T, D), bf16),
             pltpu.VMEM((ADAPTER_RANK, D), f32),
-            pltpu.VMEM((2, ADAPTER_RANK, KEY_VALUE_HEADS * D // 2), f32),
             dma((KEY_VALUE_HEADS, 2)), dma((shards,)),
             dma((KEY_VALUE_HEADS,)), dma((shards,)),
             dma((KEY_VALUE_HEADS,)), dma((shards,)),
@@ -562,7 +594,7 @@
             collective_id=0, has_side_effects=True, vmem_limit_bytes=63 * 1024 * 1024
         ),
     )(counts, offsets, adapter_hidden[0].T, keys[0], values[0], queries[0], output_gradient[0])
-    return dq[None], dk[None], dv[None], adapter
+    return settle(dq, dk, dv, adapter)
 
 
 def solution(mesh):

time: 79.1 us -> 78.5 us (level)
  local copies, waits for them, and re-layouts: 4.34 us -> 0 us
  Pallas kernels: 72.5 us -> 76.1 us
    unnamed x10 -> x0, local copies, waits for them, and re-layouts: 4.34 us -> none
    pallas_call x0 -> x1, Pallas kernels: none -> 3.58 us  [settle(): pl.pallas_call(settle_kernel, out_shape=tuple((jax.ShapeDtypeStruct((1,)...]
where the time goes in v3:
time: 78.5 us; the launch traced here: 78.2 us
  Pallas kernels  76.1 us (97%)
  between operations  2.11 us (3%)
    pallas_call x1, Pallas kernels, by_head(): pl.pallas_call(functools.partial(head_kernel, shards), out_shape=(jax.Sha...  72.5 us
    pallas_call x1, Pallas kernels, settle(): pl.pallas_call(settle_kernel, out_shape=tuple((jax.ShapeDtypeStruct((1,)...  3.58 us

profile of v3, /device:TPU:0, one launch (start us, length us, event | category | flops | bytes accessed | tf_op | source)
XLA Modules:
  0.0 78.2 jit_solution(16244360801648703642)
XLA Ops:
  1.9 72.5 %shard_map.102 = (bf16[128,2048]{1,0:T(8,128)(2,1)}, bf16[128,1024]{1,0:T(8,128)(2,1)}, bf16[128,1024]{1,0:T(8,128)(2,1)}, f32[2,16,512]{2,1,0:T(8,128)}) custom-call(s32[1,1]{1,0:T(1,128)S(6)} %copy.11.count_ref, s32[1,1]{1,0:T(1,128)S(6)} %copy.12.offset_ref, bf16[16,128]{1,0:T(8,128)(2,1)} %bitcast.11, bf16[128,1024]{1,0:T(8,128)(2,1)} %bitcast.9, ...), custom_call_target="tpu_custom_call" | custom-call | tf_op jit(solution)/shard_map/pallas_call | solution.py:556
  74.5 3.6 %shard_map.103 = (bf16[1,128,2048]{2,1,0:T(8,128)(2,1)}, bf16[1,128,1024]{2,1,0:T(8,128)(2,1)}, bf16[1,128,1024]{2,1,0:T(8,128)(2,1)}, f32[16,512]{1,0:T(8,128)}) custom-call(bf16[128,2048]{1,0:T(8,128)(2,1)} %get-tuple-element.8.dq, bf16[128,1024]{1,0:T(8,128)(2,1)} %get-tuple-element.9.dk, bf16[128,1024]{1,0:T(8,128)(2,1)} %get-tuple-element.10.dv, ...), custom_call_target="tpu_custom_call" | custom-call | tf_op jit(solution)/shard_map/pallas_call | solution.py:537
